TPU v7x, 32 devices: a whole 2x2x4 slice. The times are simulated.
32 devices in a mesh: expert: 16 (over z, y, x), dp: 2 (over core).
Axes of the slice: x: 2, y: 2, z: 4, core: 2. Of those that a mesh axis runs over, the one named last changes fastest.
Arguments:
- hidden: bfloat16 [4096, 8, 1024], P(('expert', 'dp')), may hold values from -8 to 8
- routes: int32 [4096, 8], P(('expert', 'dp')), may hold values from 0 to 15, as said below
- slots: int32 [4096, 8], P(('expert', 'dp')), may hold values from 0 to 127, as said below
- down_weight: bfloat16 [16, 1024, 7168], P('expert', None, 'dp'), may hold values from -0.1875 to 0.1875
- omega: bfloat16 [16, 1024, 256], P('expert'), may hold values from -0.1875 to 0.1875
Outputs:
- whitening: float32 [16, 1024, 1024], P('expert', 'dp')
- basis: float32 [2, 3584, 256], P('dp', 'expert')
Inputs may be any that keep to these rules, and one draw needn't show every extreme that they name: `routes`: each token names 8 different experts. Among the tokens of one device no expert is named more than 128 times, and one expert is named exactly 128 times by the tokens of every device. Among the tokens of one device, the pairs that name one expert have different slots.
All inputs are finite; a program needn't handle non-finite values.
Results may differ from a plain program's by a relative error of at most 0.0032.
Values may be sent and summed in bfloat16 or wider, within the bound.
A program may use at most 128 MiB of HBM per device.

v0:
```python
import math

import jax
import jax.numpy as jnp
from jax import lax
from jax.sharding import PartitionSpec as P

damping = 0.1
jitter = 1e-06


def contract(left, right):
    return lax.dot_general(
        left, right, (((0,), (0,)), ((), ())), preferred_element_type=jnp.float32
    )


def local(hidden, routes, slots, down_weight, omega):
    n_exp = lax.axis_size("expert")
    n_dp = lax.axis_size("dp")
    tok_rows, n_route, hid_width = hidden.shape
    capacity = 2 * tok_rows * n_route // n_exp
    n_slot = n_exp * n_dp * capacity
    slot_index = (routes * capacity + slots).reshape(-1)
    outgoing = jnp.zeros((n_exp * capacity, hid_width), jnp.bfloat16)
    outgoing = (
        outgoing.at[slot_index]
        .set(hidden.reshape(-1, hid_width))
        .reshape(n_exp, capacity, hid_width)
    )
    received = lax.all_to_all(outgoing, "expert", split_axis=0, concat_axis=0, tiled=True).reshape(
        n_exp * capacity, hid_width
    )
    gram_mat = lax.psum(contract(received, received), "dp") / n_slot
    identity_mat = jnp.eye(hid_width, dtype=jnp.float32)
    damped = gram_mat + (damping * jnp.mean(jnp.diagonal(gram_mat)) + jitter) * identity_mat
    whitening = jnp.linalg.cholesky(damped)
    test_mat = jnp.dot(
        whitening, omega[0].astype(jnp.float32), precision=lax.Precision.HIGHEST
    ).astype(jnp.bfloat16)
    down_half = down_weight[0]
    half_cols = down_half.shape[1]
    row_share = half_cols // n_exp
    whole_half = lax.psum(contract(down_half, test_mat), "expert")
    small_gram = lax.psum(jnp.dot(whole_half.T, whole_half, precision=lax.Precision.HIGHEST), "dp")
    sketch = lax.dynamic_slice_in_dim(
        whole_half, lax.axis_index("expert") * row_share, row_share, 0
    )
    qr_factor = jnp.linalg.cholesky(small_gram)
    basis_rows = jax.scipy.linalg.solve_triangular(qr_factor, sketch.T, lower=True).T * math.sqrt(
        half_cols * n_dp
    )
    own_rows = lax.dynamic_slice_in_dim(
        whitening, lax.axis_index("dp") * (hid_width // n_dp), hid_width // n_dp, 0
    )
    return (own_rows[None], basis_rows[None])


def solution(mesh):
    placed = (
        P(("expert", "dp"), None, None),
        P(("expert", "dp"), None),
        P(("expert", "dp"), None),
        P("expert", None, "dp"),
        P("expert", None, None),
    )
    return jax.shard_map(
        local,
        mesh=mesh,
        in_specs=placed,
        out_specs=(P("expert", "dp", None), P("dp", "expert", None)),
        check_vma=False,
    )
```

profile of v0, /device:TPU:0, one launch (start us, length us, event | category | flops | bytes accessed | tf_op | source)
XLA Modules:
  0.0 671.0 jit_solution(15717495369767054281)
XLA Ops:
  7.2 0.8 multiply_add_fusion
  8.8 7.9 %scatter_custom_fusion = bf16[2048,1024]{1,0:T(8,128)(2,1)} fusion(s32[1024]{0:T(1024)S(1)} %bitcast.111, bf16[128,8,1024]{2,1,0:T(8,128)(2,1)S(1)} %copy-done, bf16[]{:T(256)} %constant.347.clone.1), kind=kCustom, calls=%fused_computation.14 | custom fusion | bytes 6291458 | tf_op jit(solution)/shard_map/scatter | solution.py:28
  16.7 102.1 %all_to_all.5 = bf16[16,128,1024]{2,1,0:T(8,128)(2,1)S(1)} all-to-all(bf16[16,128,1024]{2,1,0:T(8,128)(2,1)} %bitcast.109), channel_id=1, replica_groups=mesh['expert'=16,'dp'=2] {'expert'}, dimensions={0} | all-to-all | bytes 8388608 | tf_op jit(solution)/shard_map/all_to_all | solution.py:31
  118.8 6.2 convolution_bitcast_fusion
  125.1 26.8 %all-reduce.6.cloned.1.call-done = f32[1024,1024]{0,1:T(8,128)} async-done(((f32[1024,1024]{0,1:T(8,128)}), f32[1024,1024]{0,1:T(8,128)}) %all-reduce.6.cloned.1.call-update) | async-done | bytes 4194320 | tf_op jit(solution)/shard_map/psum | solution.py:34
  151.8 5.0 broadcast_multiply_fusion
  156.8 16.8 %gather_fusion = f32[1024]{0:T(1024)S(1)} fusion(f32[1024,1024]{0,1:T(8,128)} %broadcast_multiply_fusion, s32[1024]{0:T(1024)S(1)} %bitcast.108), kind=kCustom, calls=%fused_computation | custom fusion | bytes 16384 | tf_op jit(solution)/shard_map/jit(diagonal)/cond/branch_0_fun/gather | solution.py:36
  174.9 5.0 select_add_fusion
  180.0 5.8 copy.30
  185.8 4.5 fusion.5
  190.3 1.9 copy-done.3
  192.2 11.7 %cholesky.249 = f32[128,128]{1,0:T(8,128)S(1)} custom-call(f32[128,128]{1,0:T(8,128)S(1)} %cholesky.650), custom_call_target="Cholesky" | custom-call | tf_op jit(solution)/shard_map/jit(cholesky)/cholesky | solution.py:37
  204.1 9.8 %custom-call.67 = f32[1,128,128]{1,2,0:T(8,128)S(1)} custom-call(f32[1,128,128]{2,1,0:T(8,128)S(1)} %get-tuple-element.38), custom_call_target="InvertDiagBlocksLowerTriangular" | custom-call | tf_op jit(solution)/shard_map/jit(cholesky)/cholesky | solution.py:37
  213.9 1.5 fusion.17
  215.6 1.6 convolution_subtract_fusion
  217.2 11.7 %cholesky.274 = f32[128,128]{1,0:T(8,128)S(1)} custom-call(f32[128,128]{1,0:T(8,128)S(1)} %cholesky.654), custom_call_target="Cholesky" | custom-call | tf_op jit(solution)/shard_map/jit(cholesky)/cholesky | solution.py:37
  229.2 2.5 cholesky.281
  231.7 9.8 %custom-call.68 = f32[1,128,128]{1,2,0:T(8,128)S(1)} custom-call(f32[1,128,128]{2,1,0:T(8,128)S(1)} %get-tuple-element.36), custom_call_target="InvertDiagBlocksLowerTriangular" | custom-call | tf_op jit(solution)/shard_map/jit(cholesky)/cholesky | solution.py:37
  241.5 0.8 constant_dynamic-update-slice_fusion.3
  242.9 1.3 convolution_dynamic-update-slice_fusion
  244.3 2.7 convolution_subtract_fusion.1
  247.0 11.7 %cholesky.299 = f32[128,128]{1,0:T(8,128)S(1)} custom-call(f32[128,128]{1,0:T(8,128)S(1)} %cholesky.659), custom_call_target="Cholesky" | custom-call | tf_op jit(solution)/shard_map/jit(cholesky)/cholesky | solution.py:37
  259.5 9.8 %custom-call.69 = f32[1,128,128]{1,2,0:T(8,128)S(1)} custom-call(f32[1,128,128]{2,1,0:T(8,128)S(1)} %get-tuple-element.34), custom_call_target="InvertDiagBlocksLowerTriangular" | custom-call | tf_op jit(solution)/shard_map/jit(cholesky)/cholesky | solution.py:37
  269.3 1.3 convolution_dynamic-update-slice_fusion.1
  270.5 3.3 convolution_subtract_fusion.2
  273.9 11.7 %cholesky.539 = f32[128,128]{1,0:T(8,128)S(1)} custom-call(f32[128,128]{1,0:T(8,128)S(1)} %cholesky.664), custom_call_target="Cholesky" | custom-call | tf_op jit(solution)/shard_map/jit(cholesky)/cholesky | solution.py:37
  286.4 9.8 %custom-call.70 = f32[1,128,128]{1,2,0:T(8,128)S(1)} custom-call(f32[1,128,128]{2,1,0:T(8,128)S(1)} %get-tuple-element.32), custom_call_target="InvertDiagBlocksLowerTriangular" | custom-call | tf_op jit(solution)/shard_map/jit(cholesky)/cholesky | solution.py:37
  296.2 1.1 convolution_dynamic-update-slice_fusion.2
  297.3 3.1 convolution_subtract_fusion.3
  300.5 12.1 %cholesky.558 = f32[128,128]{1,0:T(8,128)S(1)} custom-call(f32[128,128]{1,0:T(8,128)S(1)} %cholesky.669), custom_call_target="Cholesky" | custom-call | tf_op jit(solution)/shard_map/jit(cholesky)/cholesky | solution.py:37
  313.3 9.8 %custom-call.71 = f32[1,128,128]{1,2,0:T(8,128)S(1)} custom-call(f32[1,128,128]{2,1,0:T(8,128)S(1)} %get-tuple-element.30), custom_call_target="InvertDiagBlocksLowerTriangular" | custom-call | tf_op jit(solution)/shard_map/jit(cholesky)/cholesky | solution.py:37
  323.2 1.1 convolution_dynamic-update-slice_fusion.3
  324.3 3.1 convolution_subtract_fusion.4
  327.4 11.7 %cholesky.578 = f32[128,128]{1,0:T(8,128)S(1)} custom-call(f32[128,128]{1,0:T(8,128)S(1)} %cholesky.674), custom_call_target="Cholesky" | custom-call | tf_op jit(solution)/shard_map/jit(cholesky)/cholesky | solution.py:37
  339.8 9.8 %custom-call.72 = f32[1,128,128]{1,2,0:T(8,128)S(1)} custom-call(f32[1,128,128]{2,1,0:T(8,128)S(1)} %get-tuple-element.28), custom_call_target="InvertDiagBlocksLowerTriangular" | custom-call | tf_op jit(solution)/shard_map/jit(cholesky)/cholesky | solution.py:37
  349.7 1.0 convolution_dynamic-update-slice_fusion.4
  350.7 2.8 convolution_subtract_fusion.6
  353.5 11.7 %cholesky.598 = f32[128,128]{1,0:T(8,128)S(1)} custom-call(f32[128,128]{1,0:T(8,128)S(1)} %cholesky.679), custom_call_target="Cholesky" | custom-call | tf_op jit(solution)/shard_map/jit(cholesky)/cholesky | solution.py:37
  366.0 9.8 %custom-call.77 = f32[1,128,128]{1,2,0:T(8,128)S(1)} custom-call(f32[1,128,128]{2,1,0:T(8,128)S(1)} %get-tuple-element.26), custom_call_target="InvertDiagBlocksLowerTriangular" | custom-call | tf_op jit(solution)/shard_map/jit(cholesky)/cholesky/custom-call.17 | solution.py:37
  375.8 0.9 fusion.9
  376.7 2.1 convolution_subtract_fusion.8
  378.8 11.7 %cholesky.612 = f32[128,128]{1,0:T(8,128)S(1)} custom-call(f32[128,128]{1,0:T(8,128)S(1)} %convolution_subtract_fusion.8), custom_call_target="Cholesky" | custom-call | tf_op jit(solution)/shard_map/jit(cholesky)/cholesky | solution.py:37
  391.3 0.7 compare_reduce_fusion.7
  401.0 2.7 select_select_fusion
  403.8 1.9 copy-done.2
  405.7 3.6 convolution_convert_fusion
  409.3 7.1 %fusion.2 = f32[3584,256]{0,1:T(8,128)} fusion(bf16[1024,256]{1,0:T(8,128)(2,1)S(1)} %convolution_convert_fusion, bf16[1,1024,3584]{2,1,0:T(8,128)(2,1)} %param.10), kind=kOutput, calls=%fused_computation.6 | convolution fusion | flops 1879048192 | bytes 11534336 | tf_op jit(solution)/shard_map/dot_general | solution.py:13
  416.5 158.5 %all-reduce.8.cloned.1.call-done = f32[3584,256]{0,1:T(8,128)} async-done(((f32[3584,256]{0,1:T(8,128)}), f32[3584,256]{0,1:T(8,128)}) %all-reduce.8.cloned.1.call-update) | async-done | bytes 3670032 | tf_op jit(solution)/shard_map/psum | solution.py:44
  575.0 7.0 %fusion.47 = f32[256,256]{0,1:T(8,128)} fusion(f32[3584,256]{0,1:T(8,128)} %all-reduce.8.cloned.1.call-done), kind=kOutput, calls=%fused_computation.125 | convolution fusion | flops 2818572288 | bytes 3932160 | tf_op jit(solution)/shard_map/dot_general | solution.py:45
  582.0 3.3 constant_dynamic-slice_fusion.1
  585.3 3.1 copy.45
  588.4 1.1 dynamic-slice_bitcast_fusion
  589.6 9.9 %all-reduce.10.cloned.1.call-done = f32[256,256]{0,1:T(8,128)} async-done(((f32[256,256]{0,1:T(8,128)}), f32[256,256]{0,1:T(8,128)}) %all-reduce.10.cloned.1.call-update) | async-done | bytes 262160 | tf_op jit(solution)/shard_map/psum | solution.py:45
  599.5 1.1 copy.47
  600.5 1.0 fusion.25
  601.6 11.7 %cholesky.625 = f32[128,128]{1,0:T(8,128)S(1)} custom-call(f32[128,128]{1,0:T(8,128)S(1)} %cholesky.683), custom_call_target="Cholesky" | custom-call | tf_op jit(solution)/shard_map/jit(cholesky)/cholesky | solution.py:49
  613.3 9.8 %custom-call.78 = f32[1,128,128]{1,2,0:T(8,128)S(1)} custom-call(f32[1,128,128]{2,1,0:T(8,128)S(1)} %get-tuple-element.24), custom_call_target="InvertDiagBlocksLowerTriangular" | custom-call | tf_op jit(solution)/shard_map/jit(cholesky)/cholesky/custom-call.17 | solution.py:49
  623.6 11.7 %cholesky.634 = f32[128,128]{1,0:T(8,128)S(1)} custom-call(f32[128,128]{1,0:T(8,128)S(1)} %convolution_subtract_fusion.7), custom_call_target="Cholesky" | custom-call | tf_op jit(solution)/shard_map/jit(cholesky)/cholesky | solution.py:49
  635.3 0.7 compare_reduce_fusion.1
  638.1 4.1 while.1
  638.8 1.3 bitcast_dynamic-update-slice_fusion.2
  640.8 1.3 bitcast_dynamic-update-slice_fusion.2
  642.1 20.0 %custom-call.73 = f32[2,128,128]{1,2,0:T(8,128)S(1)} custom-call(f32[2,128,128]{2,1,0:T(8,128)S(1)} %get-tuple-element.10), custom_call_target="InvertDiagBlocksLowerTriangular" | custom-call | tf_op jit(solution)/shard_map/jit(_solve_triangular)/triangular_solve | solution.py:50
  663.3 0.7 fusion.26
  (74 shorter events, 15.2 us)
Async XLA Ops:
  7.2 1.6 copy-start
  7.2 144.7 %all-reduce.6.cloned.1.call-start = ((), (), s32[]{:S(2)}) async-start(), calls=%async_computation.1 | async-start | bytes 8388608 | tf_op jit(solution)/shard_map/psum | solution.py:34
  125.0 450.0 %all-reduce.8.cloned.1.call-start = ((), (), s32[]{:S(2)}) async-start(), calls=%async_computation.2 | async-start | bytes 7340032 | tf_op jit(solution)/shard_map/psum | solution.py:44
  190.3 1.9 copy-start.3
  401.0 4.7 copy-start.4
  403.8 1.9 copy-start.2
  416.5 183.0 %all-reduce.10.cloned.1.call-start = ((), (), s32[]{:S(2)}) async-start(), calls=%async_computation.3 | async-start | bytes 524288 | tf_op jit(solution)/shard_map/psum | solution.py:45
  582.0 82.0 %copy-start.1 = (bf16[128,8,1024]{2,1,0:T(8,128)(2,1)S(1)}, bf16[128,8,1024]{2,1,0:T(8,128)(2,1)}, u32[]{:S(2)}) copy-start(bf16[128,8,1024]{2,1,0:T(8,128)(2,1)} %param.7) | copy-start | bytes 6291460
Sparse Core Ops, SparseCore 0:
  125.1 26.6 all-reduce.5
  416.6 158.3 all-reduce.7
  582.1 17.3 all-reduce.9
where the time goes:
time: 679 us; the launch traced here: 671 us
  other arithmetic  243 us (36%)
  waiting for transfers between devices  195 us (29%)
  blocking collectives  102 us (15%)
  local copies, waits for them, and re-layouts  56.8 us (8%)
  matrix products  52.5 us (8%)
  between operations  21.6 us (3%)
    another operation x30, other arithmetic, local(): whitening = jnp.linalg.cholesky(damped)  168 us
    psum x1, waiting for transfers between devices, local(): whole_half = lax.psum(contract(down_half, test_mat), 'expert')  158 us
    all_to_all x1, blocking collectives, local(): lax.all_to_all(outgoing, 'expert', split_axis=0, concat_axis=0, tiled=True)  102 us
    another operation x7, other arithmetic, local(): qr_factor = jnp.linalg.cholesky(small_gram)  34.6 us
    another operation x14, matrix products, local(): whitening = jnp.linalg.cholesky(damped)  27 us
    psum x1, waiting for transfers between devices, local(): gram_mat = lax.psum(contract(received, received), 'dp') / n_slot  26.8 us
    another operation x3, other arithmetic, local(): jax.scipy.linalg.solve_triangular(qr_factor, sketch.T, lower=True)  20 us
    gather x1, local copies, waits for them, and re-layouts, local(): jnp.diagonal(gram_mat)  16.8 us
  transfers between devices with their start and end apart: 3, of which 3 were waited for; matrix products, arithmetic and copies ran while one was open for 1% of the time, Pallas kernels for 0%

commit v1 on v0

v1 whole, which is shorter than its diff:
```python
import functools
import math

import jax
import jax.numpy as jnp
from jax import lax
from jax.experimental import pallas as pl
from jax.experimental.pallas import tpu as pltpu
from jax.sharding import PartitionSpec as P

damping = 0.1
jitter = 1e-06
BLK = 128
PANEL = 4
HIGH = lax.Precision.HIGHEST


def contract(left, right):
    return lax.dot_general(
        left, right, (((0,), (0,)), ((), ())), preferred_element_type=jnp.float32
    )


def dot_nt(left, right):
    return lax.dot_general(
        left, right, (((1,), (1,)), ((), ())),
        precision=HIGH, preferred_element_type=jnp.float32,
    )


def factor_block(block):
    tiles = [block[r:r + 8] for r in range(0, BLK, 8)]
    row_id = lax.broadcasted_iota(jnp.int32, (8, BLK), 0)
    lane_id = lax.broadcasted_iota(jnp.int32, (8, BLK), 1)
    inv_tiles = [
        jnp.where(row_id + r == lane_id, 1.0, 0.0).astype(jnp.float32)
        for r in range(0, BLK, 8)
    ]
    n_tile = BLK // 8
    for start in range(0, BLK, PANEL):
        first = start // 8
        off = start % 8
        cols = [
            {t: jnp.broadcast_to(tiles[t][:, start + m:start + m + 1], (8, BLK))
             for t in range(first, n_tile)}
            for m in range(PANEL)
        ]
        rows = [tiles[first][off + m:off + m + 1] for m in range(PANEL)]
        inv_rows = [inv_tiles[first][off + m:off + m + 1] for m in range(PANEL)]
        for m in range(PANEL):
            pivot = cols[m][first][off + m:off + m + 1]
            recip = 1.0 / pivot
            for t in range(first, n_tile):
                cols[m][t] = cols[m][t] * recip
            cols[m][first] = jnp.where(row_id > off + m, cols[m][first], 0.0)
            for n in range(m + 1, PANEL):
                scale = cols[n][first][off + m:off + m + 1]
                ratio = cols[m][first][off + n:off + n + 1]
                for t in range(first, n_tile):
                    cols[n][t] = cols[n][t] - cols[m][t] * scale
                rows[n] = rows[n] - ratio * rows[m]
                inv_rows[n] = inv_rows[n] - ratio * inv_rows[m]
        for t in range(first, n_tile):
            a, b = tiles[t], inv_tiles[t]
            for m in range(PANEL):
                a = a - cols[m][t] * rows[m]
                b = b - cols[m][t] * inv_rows[m]
            tiles[t], inv_tiles[t] = a, b
    upper, inverse = [], []
    for t in range(n_tile):
        diag = row_id + t * 8 == lane_id
        pivots = jnp.sum(jnp.where(diag, tiles[t], 0.0), axis=1, keepdims=True)
        scale = 1.0 / jnp.sqrt(pivots)
        upper.append(jnp.where(row_id + t * 8 <= lane_id, tiles[t] * scale, 0.0))
        inverse.append(inv_tiles[t] * scale)
    return jnp.concatenate(upper, 0).T, jnp.concatenate(inverse, 0)


def diagonal_mask():
    return lax.broadcasted_iota(jnp.int32, (BLK, BLK), 0) == lax.broadcasted_iota(
        jnp.int32, (BLK, BLK), 1
    )


def whiten_kernel(n_slot, top_a, top_b, low_a, low_b, out):
    width = out.shape[0]
    half = width // 2
    n_blk = width // BLK
    scale = 1.0 / n_slot
    out[:half, :half] = (top_a[...] + top_b[...]) * scale
    out[half:, :] = (low_a[...] + low_b[...]) * scale
    eye = diagonal_mask()
    total = jnp.zeros((BLK, BLK), jnp.float32)
    for k in range(n_blk):
        s = slice(k * BLK, (k + 1) * BLK)
        total = total + jnp.where(eye, out[s, s], 0.0)
    mean = jnp.sum(jnp.sum(total, axis=0, keepdims=True), axis=1, keepdims=True) / width
    shift = jnp.where(eye, damping * mean + jitter, 0.0)
    for k in range(n_blk):
        s = slice(k * BLK, (k + 1) * BLK)
        out[s, s] += shift

    @pl.loop(0, n_blk)
    def _(k):
        here = pl.ds(pl.multiple_of(k * BLK, BLK), BLK)
        lower, inverse = factor_block(out[here, here])
        out[here, here] = lower
        for kk in range(n_blk - 1):
            @pl.when(k == kk)
            def _():
                rest = (kk + 1) * BLK
                panel = dot_nt(out[rest:, kk * BLK:rest], inverse)
                out[rest:, kk * BLK:rest] = panel
                for j in range(kk + 1, n_blk):
                    part = panel[j * BLK - rest:]
                    out[j * BLK:, j * BLK:(j + 1) * BLK] -= dot_nt(part, part[:BLK])

    for k in range(n_blk - 1):
        out[k * BLK:(k + 1) * BLK, (k + 1) * BLK:] = jnp.zeros(
            (BLK, width - (k + 1) * BLK), jnp.float32
        )


def basis_kernel(root, gram, sketch, out, work, inv):
    rank = gram.shape[0]
    n_blk = rank // BLK
    work[...] = gram[...]

    @pl.loop(0, n_blk)
    def _(k):
        here = pl.ds(pl.multiple_of(k * BLK, BLK), BLK)
        _, inverse = factor_block(work[here, here])
        inv[here, :] = inverse
        for kk in range(n_blk - 1):
            @pl.when(k == kk)
            def _():
                rest = (kk + 1) * BLK
                panel = dot_nt(work[rest:, kk * BLK:rest], inverse)
                work[rest:, kk * BLK:rest] = panel
                for j in range(kk + 1, n_blk):
                    part = panel[j * BLK - rest:]
                    work[j * BLK:, j * BLK:(j + 1) * BLK] -= dot_nt(part, part[:BLK])

    for k in range(n_blk):
        s = slice(k * BLK, (k + 1) * BLK)
        right = sketch[:, s]
        for j in range(k):
            t = slice(j * BLK, (j + 1) * BLK)
            right = right - dot_nt(out[:, t], work[s, t])
        out[:, s] = dot_nt(right, inv[s, :])
    out[...] = out[...] * root


def whiten(n_slot, top_a, top_b, low_a, low_b):
    width = low_a.shape[1]
    return pl.pallas_call(
        functools.partial(whiten_kernel, n_slot),
        out_shape=jax.ShapeDtypeStruct((width, width), jnp.float32),
        in_specs=[pl.BlockSpec(memory_space=pltpu.VMEM)] * 4,
        out_specs=pl.BlockSpec(memory_space=pltpu.VMEM),
        compiler_params=pltpu.CompilerParams(vmem_limit_bytes=40 * 2**20),
    )(top_a, top_b, low_a, low_b)


def finish(root, gram, sketch):
    rank = gram.shape[0]
    return pl.pallas_call(
        functools.partial(basis_kernel, root),
        out_shape=jax.ShapeDtypeStruct(sketch.shape, jnp.float32),
        in_specs=[pl.BlockSpec(memory_space=pltpu.VMEM)] * 2,
        out_specs=pl.BlockSpec(memory_space=pltpu.VMEM),
        scratch_shapes=[
            pltpu.VMEM((rank, rank), jnp.float32),
            pltpu.VMEM((rank, BLK), jnp.float32),
        ],
        compiler_params=pltpu.CompilerParams(vmem_limit_bytes=32 * 2**20),
    )(gram, sketch)


def local(hidden, routes, slots, down_weight, omega):
    n_exp = lax.axis_size("expert")
    n_dp = lax.axis_size("dp")
    tok_rows, n_route, hid_width = hidden.shape
    capacity = 2 * tok_rows * n_route // n_exp
    n_slot = n_exp * n_dp * capacity
    slot_index = (routes * capacity + slots).reshape(-1)
    outgoing = jnp.zeros((n_exp * capacity, hid_width), jnp.bfloat16)
    outgoing = (
        outgoing.at[slot_index]
        .set(hidden.reshape(-1, hid_width))
        .reshape(n_exp, capacity, hid_width)
    )
    received = lax.all_to_all(outgoing, "expert", split_axis=0, concat_axis=0, tiled=True).reshape(
        n_exp * capacity, hid_width
    )
    half = hid_width // 2
    swap = [(0, 1), (1, 0)]
    low = contract(received[:, half:], received)
    low_other = lax.ppermute(low, "dp", swap)
    top = contract(received[:, :half], received[:, :half])
    top_other = lax.ppermute(top, "dp", swap)
    whitening = whiten(n_slot, top, top_other, low, low_other)
    test_mat = jnp.dot(
        whitening, omega[0].astype(jnp.float32), precision=HIGH
    ).astype(jnp.bfloat16)
    down_half = down_weight[0]
    half_cols = down_half.shape[1]
    sketch = lax.psum_scatter(
        contract(down_half, test_mat), "expert", scatter_dimension=0, tiled=True
    )
    small_gram = lax.psum(
        lax.dot_general(sketch, sketch, (((0,), (0,)), ((), ())), precision=HIGH),
        ("expert", "dp"),
    )
    basis_rows = finish(math.sqrt(half_cols * n_dp), small_gram, sketch)
    own_rows = lax.dynamic_slice_in_dim(
        whitening, lax.axis_index("dp") * (hid_width // n_dp), hid_width // n_dp, 0
    )
    return (own_rows[None], basis_rows[None])


def solution(mesh):
    placed = (
        P(("expert", "dp"), None, None),
        P(("expert", "dp"), None),
        P(("expert", "dp"), None),
        P("expert", None, "dp"),
        P("expert", None, None),
    )
    return jax.shard_map(
        local,
        mesh=mesh,
        in_specs=placed,
        out_specs=(P("expert", "dp", None), P("dp", "expert", None)),
        check_vma=False,
    )
```

time: 679 us -> 430 us (0.63); the launches traced: 671 us -> 430 us
  other arithmetic: 243 us -> 0.86 us
  Pallas kernels: 0 us -> 73.4 us
  local copies, waits for them, and re-layouts: 56.8 us -> 14.7 us
  matrix products: 52.5 us -> 12.8 us
  waiting for transfers between devices: 195 us -> 211 us
  between operations: 21.6 us -> 14.1 us
    another operation x40 -> x0, other arithmetic: 222 us -> none  [the longest x30 168 us: local(): whitening = jnp.linalg.cholesky(damped)]
    reduce_scatter x0 -> x1, waiting for transfers between devices: none -> 84.2 us  [local(): lax.psum_scatter(contract(down_half, test_mat), 'expert', scatter_dimensi...]
    pallas_call x0 -> x2, Pallas kernels: none -> 73.4 us  [the longest x1 59.4 us: whiten(): pl.pallas_call(functools.partial(whiten_kernel, n_slot), out_shape=jax.Sh...]
    psum x3 -> x1, waiting for transfers between devices: 195 us -> 123 us  [local(): lax.psum(lax.dot_general(sketch, sketch, (((0,), (0,)), ((), ())), precis...]
    another operation x19 -> x0, matrix products: 28.6 us -> none  [the longest x14 27 us: local(): whitening = jnp.linalg.cholesky(damped)]
    gather x1 -> x0, local copies, waits for them, and re-layouts: 16.8 us -> none  [local(): jnp.diagonal(gram_mat)]
    another operation x34 -> x0, local copies, waits for them, and re-layouts: 13.1 us -> none  [the longest x25 8.94 us: local(): whitening = jnp.linalg.cholesky(damped)]
    div x3 -> x0, other arithmetic: 10.4 us -> none  [the longest x1 5 us: local(): gram_mat = lax.psum(contract(received, received), 'dp') / n_slot]
  transfers between devices with their start and end apart: 3 -> 4, of which waited for: 3 -> 3; matrix products, arithmetic and copies ran while one was open for 1% -> 1% of each run, Pallas kernels for 0% -> 0%
where the time goes in v1:
time: 430 us
  waiting for transfers between devices  211 us (49%)
  blocking collectives  102 us (24%)
  Pallas kernels  73.4 us (17%)
  local copies, waits for them, and re-layouts  14.7 us (3%)
  between operations  14.1 us (3%)
  matrix products  12.8 us (3%)
    psum x1, waiting for transfers between devices, local(): lax.psum(lax.dot_general(sketch, sketch, (((0,), (0,)), ((), ())), precis...  123 us
    all_to_all x1, blocking collectives, local(): lax.all_to_all(outgoing, 'expert', split_axis=0, concat_axis=0, tiled=True)  102 us
    reduce_scatter x1, waiting for transfers between devices, local(): lax.psum_scatter(contract(down_half, test_mat), 'expert', scatter_dimensi...  84.2 us
    pallas_call x1, Pallas kernels, whiten(): pl.pallas_call(functools.partial(whiten_kernel, n_slot), out_shape=jax.Sh...  59.4 us
    pallas_call x1, Pallas kernels, finish(): pl.pallas_call(functools.partial(basis_kernel, root), out_shape=jax.Shape...  14 us
  transfers between devices with their start and end apart: 4, of which 3 were waited for; matrix products, arithmetic and copies ran while one was open for 1% of the time, Pallas kernels for 0%

profile of v1, /device:TPU:0, one launch (start us, length us, event | category | flops | bytes accessed | tf_op | source)
XLA Modules:
  0.0 430.1 jit_solution(12351643972599260681)
XLA Ops:
  7.2 0.0 copy-start
  7.2 0.0 reduce-scatter.2.cloned.1.call-start
  7.2 0.8 multiply_add_fusion
  8.1 0.1 copy.8
  8.2 0.1 reshape.44
  8.3 0.5 copy-done
  8.8 7.9 %scatter_custom_fusion = bf16[2048,1024]{1,0:T(8,128)(2,1)} fusion(s32[1024]{0:T(1024)S(1)} %bitcast.28, bf16[128,8,1024]{2,1,0:T(8,128)(2,1)S(1)} %copy-done, bf16[]{:T(256)} %constant.7.clone.1), kind=kCustom, calls=%fused_computation.8 | custom fusion | bytes 6291458 | tf_op jit(solution)/shard_map/scatter | solution.py:190
  16.7 102.1 %all_to_all.5 = bf16[16,128,1024]{2,1,0:T(8,128)(2,1)S(1)} all-to-all(bf16[16,128,1024]{2,1,0:T(8,128)(2,1)} %bitcast.24), channel_id=1, replica_groups=mesh['expert'=16,'dp'=2] {'expert'}, dimensions={0} | all-to-all | bytes 8388608 | tf_op jit(solution)/shard_map/all_to_all | solution.py:193
  118.8 2.4 fusion.5.low_a
  121.2 0.1 collective-permute-start.1
  121.2 0.0 slice-start
  121.2 1.3 fusion.7.top_a
  122.5 0.0 copy-start.4
  122.5 0.0 slice-start.1
  122.6 0.5 collective-permute-start
  123.1 3.8 collective-permute-done.top_b
  126.9 0.0 collective-permute-done.1.low_b
  126.9 59.4 %shard_map.68 = f32[1024,1024]{1,0:T(8,128)S(1)} custom-call(f32[512,512]{1,0:T(8,128)S(1)} %fusion.7.top_a, f32[512,512]{1,0:T(8,128)S(1)} %collective-permute-done.top_b, f32[512,1024]{1,0:T(8,128)S(1)} %fusion.5.low_a, f32[512,1024]{1,0:T(8,128)S(1)} %collective-permute-done.1.low_b), custom_call_target="tpu_custom_call" | custom-call | tf_op jit(solution)/shard_map/pallas_call | solution.py:156
  186.3 0.0 copy-start.1
  186.3 1.9 copy-done.1
  188.3 0.0 copy-done.4
  188.3 2.0 convolution_convert_fusion
  190.3 0.0 slice-done
  190.3 0.0 slice-done.1
  190.3 4.8 %fusion.2 = f32[3584,256]{1,0:T(8,128)} fusion(bf16[1024,256]{1,0:T(8,128)(2,1)S(1)} %convolution_convert_fusion, bf16[1,1024,3584]{2,1,0:T(8,128)(2,1)S(1)} %bitcast.30), kind=kOutput, calls=%fused_computation.3 | convolution fusion | flops 1879048192 | bytes 11534336 | tf_op jit(solution)/shard_map/dot_general | solution.py:19
  195.1 0.0 reduce-scatter.2.cloned.1.call-update
  195.1 0.0 all-reduce.2.cloned.1.call-start
  195.2 84.2 %reduce-scatter.2.cloned.1.call-done.sketch = f32[224,256]{1,0:T(8,128)} async-done(((f32[3584,256]{1,0:T(8,128)}), f32[224,256]{1,0:T(8,128)}) %reduce-scatter.2.cloned.1.call-update) | async-done | bytes 229392 | tf_op jit(solution)/shard_map/reduce_scatter | solution.py:208
  279.4 0.0 copy-start.2
  279.4 2.4 fusion.13
  281.8 0.0 all-reduce.2.cloned.1.call-update
  281.8 3.2 dynamic-slice_bitcast_fusion
  285.0 123.4 %all-reduce.2.cloned.1.call-done.gram = f32[256,256]{1,0:T(8,128)} async-done(((f32[256,256]{1,0:T(8,128)}), f32[256,256]{1,0:T(8,128)}) %all-reduce.2.cloned.1.call-update) | async-done | bytes 262160 | tf_op jit(solution)/shard_map/psum | solution.py:211
  408.3 0.0 copy-done.2
  408.3 0.0 copy-start.3
  408.3 0.9 copy-done.3
  409.3 14.0 %shard_map.69 = f32[224,256]{1,0:T(8,128)} custom-call(f32[256,256]{1,0:T(8,128)S(1)} %copy-done.3, f32[224,256]{1,0:T(8,128)S(1)} %copy-done.2), custom_call_target="tpu_custom_call" | custom-call | tf_op jit(solution)/shard_map/pallas_call | solution.py:167
  (2 shorter events, 0.0 us)
Async XLA Ops:
  7.2 1.6 copy-start
  7.2 272.2 %reduce-scatter.2.cloned.1.call-start = ((), (), s32[]{:S(2)}) async-start(), calls=%async_computation.2 | async-start | bytes 3899392 | tf_op jit(solution)/shard_map/reduce_scatter | solution.py:208
  121.2 5.7 %collective-permute-start.1 = (f32[512,1024]{1,0:T(8,128)S(1)}, f32[512,1024]{1,0:T(8,128)S(1)}, u32[]{:S(2)}, u32[]{:S(2)}) collective-permute-start(f32[512,1024]{1,0:T(8,128)S(1)} %fusion.5.low_a), channel_id=1, source_target_pairs={{0,1},{1,0},{2,3},{3,2},{4,5},{5,4},{6,7},{7,6},{8,9},{9,8},{10,11... | collective-permute-start | bytes 6291464 | tf_op jit(solution)/shard_map/ppermute | solution.py:199
  121.2 69.1 %slice-start = ((s8[7340032]{0:T(1024)(128)(4,1)}), s8[4194304]{0:T(1024)(128)(4,1)S(1)}, s32[]{:S(2)}) async-start(s8[7340032]{0:T(1024)(128)(4,1)} %bitcast.29), calls=%async_computation.4 | async-start | bytes 8388608
  122.5 65.7 %copy-start.4 = (bf16[1,1024,256]{2,1,0:T(8,128)(2,1)S(1)}, bf16[1,1024,256]{2,1,0:T(8,128)(2,1)}, u32[]{:S(2)}) copy-start(bf16[1,1024,256]{2,1,0:T(8,128)(2,1)} %param.9) | copy-start | bytes 1572868
  122.5 67.8 %slice-start.1 = ((s8[7340032]{0:T(1024)(128)(4,1)}), s8[3145728]{0:T(1024)(128)(4,1)S(1)}, s32[]{:S(2)}) async-start(s8[7340032]{0:T(1024)(128)(4,1)} %bitcast.29), calls=%async_computation.5 | async-start | bytes 6291456
  122.6 4.3 %collective-permute-start = (f32[512,512]{1,0:T(8,128)S(1)}, f32[512,512]{1,0:T(8,128)S(1)}, u32[]{:S(2)}, u32[]{:S(2)}) collective-permute-start(f32[512,512]{1,0:T(8,128)S(1)} %fusion.7.top_a), channel_id=1, source_target_pairs={{0,1},{1,0},{2,3},{3,2},{4,5},{5,4},{6,7},{7,6},{8,9},{9,8},{10,11... | collective-permute-start | bytes 3145736 | tf_op jit(solution)/shard_map/ppermute | solution.py:201
  186.3 1.9 copy-start.1
  195.1 213.2 %all-reduce.2.cloned.1.call-start = ((), (), s32[]{:S(2)}) async-start(), calls=%async_computation.3 | async-start | bytes 524288 | tf_op jit(solution)/shard_map/psum | solution.py:211
  279.4 129.0 %copy-start.2 = (f32[224,256]{1,0:T(8,128)S(1)}, f32[224,256]{1,0:T(8,128)}, u32[]{:S(2)}) copy-start(f32[224,256]{1,0:T(8,128)} %reduce-scatter.2.cloned.1.call-done.sketch) | copy-start | bytes 688132
  408.3 1.0 copy-start.3
Sparse Core Ops, SparseCore 0:
  195.2 84.0 reduce-scatter.1
  284.9 123.4 all-reduce.1

commit v2 on v1

--- a/solution.py
+++ b/solution.py
@@ -11,7 +11,7 @@
 damping = 0.1
 jitter = 1e-06
 BLK = 128
-PANEL = 4
+PANEL = 8
 HIGH = lax.Precision.HIGHEST
 
 
@@ -177,6 +177,51 @@
     )(gram, sketch)
 
 
+def exchange(parts, bit, axis):
+    mine = (lax.axis_index("expert") // bit) % 2
+    pairs = [(i, i ^ bit) for i in range(lax.axis_size("expert"))]
+    sent = lax.dynamic_index_in_dim(parts, 1 - mine, axis, keepdims=False)
+    kept = lax.dynamic_index_in_dim(parts, mine, axis, keepdims=False)
+    return kept, lax.ppermute(sent, "expert", pairs)
+
+
+def scatter_sum(down_half, test_mat, n_exp):
+    half_cols = down_half.shape[1]
+    share = half_cols // n_exp
+    rank = test_mat.shape[1]
+    outer = n_exp // 4
+    cut = half_cols // 2
+    shape = (outer // 2, 2, 2, share, rank)
+    first = contract(down_half[:, :cut], test_mat).reshape(shape)
+    first_kept, first_came = exchange(first, 1, 2)
+    second = contract(down_half[:, cut:], test_mat).reshape(shape)
+    second_kept, second_came = exchange(second, 2, 1)
+    first = first_kept + first_came
+    first_kept, first_came = exchange(first, 2, 1)
+    second = second_kept + second_came
+    second_kept, second_came = exchange(second, 1, 1)
+    quarter = jnp.concatenate([first_kept + first_came, second_kept + second_came], 0)
+    groups = [[r + 4 * h for h in range(outer)] for r in range(4)]
+    terms = lax.all_to_all(
+        quarter, "expert", split_axis=0, concat_axis=0, axis_index_groups=groups, tiled=True
+    )
+    return jnp.sum(terms, 0)
+
+
+def gram_over_all(sketch, n_exp, swap):
+    rank = sketch.shape[1]
+    partial = lax.dot_general(sketch, sketch, (((0,), (0,)), ((), ())), precision=HIGH)
+    pieces = partial.reshape(n_exp, rank // n_exp, rank)
+    own = jnp.sum(
+        lax.all_to_all(pieces, "expert", split_axis=0, concat_axis=0, tiled=True), 0
+    )
+    own = own + lax.ppermute(own, "dp", swap)
+    copies = jnp.broadcast_to(own[None], pieces.shape)
+    return lax.all_to_all(
+        copies, "expert", split_axis=0, concat_axis=0, tiled=True
+    ).reshape(rank, rank)
+
+
 def local(hidden, routes, slots, down_weight, omega):
     n_exp = lax.axis_size("expert")
     n_dp = lax.axis_size("dp")
@@ -205,13 +250,8 @@
     ).astype(jnp.bfloat16)
     down_half = down_weight[0]
     half_cols = down_half.shape[1]
-    sketch = lax.psum_scatter(
-        contract(down_half, test_mat), "expert", scatter_dimension=0, tiled=True
-    )
-    small_gram = lax.psum(
-        lax.dot_general(sketch, sketch, (((0,), (0,)), ((), ())), precision=HIGH),
-        ("expert", "dp"),
-    )
+    sketch = scatter_sum(down_half, test_mat, n_exp)
+    small_gram = gram_over_all(sketch, n_exp, swap)
     basis_rows = finish(math.sqrt(half_cols * n_dp), small_gram, sketch)
     own_rows = lax.dynamic_slice_in_dim(
         whitening, lax.axis_index("dp") * (hid_width // n_dp), hid_width // n_dp, 0

time: 430 us -> 289 us (0.67)
  waiting for transfers between devices: 211 us -> 41.9 us
  blocking collectives: 102 us -> 137 us
  Pallas kernels: 73.4 us -> 57.4 us
  between operations: 14.1 us -> 0.77 us
  local copies, waits for them, and re-layouts: 14.7 us -> 24.5 us
  starting transfers between devices: 0.7 us -> 7.69 us
    psum x1 -> x0, waiting for transfers between devices: 123 us -> none  [local(): lax.psum(lax.dot_general(sketch, sketch, (((0,), (0,)), ((), ())), precis...]
    reduce_scatter x1 -> x0, waiting for transfers between devices: 84.2 us -> none  [local(): lax.psum_scatter(contract(down_half, test_mat), 'expert', scatter_dimensi...]
    all_to_all x0 -> x2, blocking collectives: none -> 34.7 us  [the longest x1 23.5 us: scatter_sum(): lax.all_to_all(quarter, 'expert', split_axis=0, concat_axis=0, axis_index...]
    ppermute x0 -> x5, waiting for transfers between devices: none -> 30.9 us  [the longest x4 29.7 us: exchange(): return (kept, lax.ppermute(sent, 'expert', pairs))]
    pallas_call x1, Pallas kernels: 59.4 us -> 47.2 us  [whiten(): pl.pallas_call(functools.partial(whiten_kernel, n_slot), out_shape=jax.Sh...]
    all_to_all x0 -> x1, waiting for transfers between devices: none -> 7.05 us  [gram_over_all(): lax.all_to_all(copies, 'expert', split_axis=0, concat_axis=0, tiled=True)]
    dot_general x0 -> x3, local copies, waits for them, and re-layouts: none -> 5.6 us  [the longest x2 5.47 us: contract(): lax.dot_general(left, right, (((0,), (0,)), ((), ())), preferred_element_...]
    dot_general x3 -> x4, matrix products: 8.41 us -> 13.8 us  [contract(): lax.dot_general(left, right, (((0,), (0,)), ((), ())), preferred_element_...]
  transfers between devices with their start and end apart: 4 -> 8, of which waited for: 3 -> 7; matrix products, arithmetic and copies ran while one was open for 1% -> 5% of each run, Pallas kernels for 0% -> 0%
where the time goes in v2:
time: 289 us; the launch traced here: 288 us
  blocking collectives  137 us (47%)
  Pallas kernels  57.4 us (20%)
  waiting for transfers between devices  41.9 us (14%)
  local copies, waits for them, and re-layouts  24.5 us (8%)
  matrix products  16.2 us (6%)
  starting transfers between devices  7.69 us (3%)
    all_to_all x1, blocking collectives, local(): lax.all_to_all(outgoing, 'expert', split_axis=0, concat_axis=0, tiled=True)  102 us
    pallas_call x1, Pallas kernels, whiten(): pl.pallas_call(functools.partial(whiten_kernel, n_slot), out_shape=jax.Sh...  47.2 us
    ppermute x4, waiting for transfers between devices, exchange(): return (kept, lax.ppermute(sent, 'expert', pairs))  29.7 us
    all_to_all x1, blocking collectives, scatter_sum(): lax.all_to_all(quarter, 'expert', split_axis=0, concat_axis=0, axis_index...  23.5 us
    dot_general x4, matrix products, contract(): lax.dot_general(left, right, (((0,), (0,)), ((), ())), preferred_element_...  13.8 us
    all_to_all x1, blocking collectives, gram_over_all(): lax.all_to_all(pieces, 'expert', split_axis=0, concat_axis=0, tiled=True)  11.2 us
    pallas_call x1, Pallas kernels, finish(): pl.pallas_call(functools.partial(basis_kernel, root), out_shape=jax.Shape...  10.3 us
    scatter x1, local copies, waits for them, and re-layouts, local(): outgoing = outgoing.at[slot_index].set(hidden.reshape(-1, hid_width)).res...  7.89 us
  transfers between devices with their start and end apart: 8, of which 7 were waited for; matrix products, arithmetic and copies ran while one was open for 5% of the time, Pallas kernels for 0%

profile of v2, /device:TPU:0, one launch (start us, length us, event | category | flops | bytes accessed | tf_op | source)
XLA Modules:
  0.0 288.1 jit_solution(7864983635423872863)
XLA Ops:
  0.6 0.0 copy-start
  0.6 0.9 multiply_add_fusion
  1.5 0.1 copy.12
  1.6 0.1 reshape.56
  1.7 0.5 copy-done
  2.3 7.9 %scatter_custom_fusion = bf16[2048,1024]{1,0:T(8,128)(2,1)} fusion(s32[1024]{0:T(1024)S(1)} %bitcast.57, bf16[128,8,1024]{2,1,0:T(8,128)(2,1)S(1)} %copy-done, bf16[]{:T(256)} %constant.79.clone.1), kind=kCustom, calls=%fused_computation.11 | custom fusion | bytes 6291458 | tf_op jit(solution)/shard_map/scatter | solution.py:235
  10.1 102.1 %all_to_all.20 = bf16[16,128,1024]{2,1,0:T(8,128)(2,1)S(1)} all-to-all(bf16[16,128,1024]{2,1,0:T(8,128)(2,1)} %bitcast.48), channel_id=1, replica_groups=mesh['expert'=16,'dp'=2] {'expert'}, dimensions={0} | all-to-all | bytes 8388608 | tf_op jit(solution)/shard_map/all_to_all | solution.py:238
  112.2 3.7 %fusion.10.low_a = f32[512,1024]{1,0:T(8,128)} fusion(bf16[2048,1024]{1,0:T(8,128)(2,1)S(1)} %bitcast.53), kind=kOutput, calls=%fused_computation.7 | convolution fusion | flops 2147483648 | bytes 8388608 | tf_op jit(solution)/shard_map/dot_general | solution.py:19
  115.9 0.0 collective-permute-start.1
  115.9 1.3 fusion.12.top_a
  117.2 0.6 collective-permute-start
  117.8 0.0 copy-start.3
  117.8 3.9 %collective-permute-done.top_b = f32[512,512]{1,0:T(8,128)} collective-permute-done((f32[512,512]{1,0:T(8,128)S(1)}, f32[512,512]{1,0:T(8,128)}, u32[]{:S(2)}, u32[]{:S(2)}) %collective-permute-start) | collective-permute-done | bytes 1048608 | tf_op jit(solution)/shard_map/ppermute | solution.py:246
  121.7 0.0 collective-permute-done.1.low_b
  121.7 47.2 %shard_map.68 = f32[1024,1024]{1,0:T(8,128)S(1)} custom-call(f32[512,512]{1,0:T(8,128)S(1)} %fusion.12.top_a, f32[512,512]{1,0:T(8,128)} %collective-permute-done.top_b, f32[512,1024]{1,0:T(8,128)} %fusion.10.low_a, f32[512,1024]{1,0:T(8,128)} %collective-permute-done.1.low_b), custom_call_target="tpu_custom_call" | custom-call | tf_op jit(solution)/shard_map/pallas_call | solution.py:156
  168.9 0.0 copy-start.1
  168.9 1.9 copy-done.1
  170.8 0.0 copy-done.3
  170.8 2.0 convolution_convert_fusion
  172.9 4.4 %fusion.7 = f32[1792,256]{0,1:T(8,128)} fusion(bf16[1024,256]{1,0:T(8,128)(2,1)S(1)} %convolution_convert_fusion, bf16[1024,3584]{1,0:T(8,128)(2,1)} %bitcast.58), kind=kOutput, calls=%fused_computation.6 | convolution fusion | flops 939524096 | bytes 6029312 | tf_op jit(solution)/shard_map/dot_general | solution.py:19
  177.3 2.8 copy.14
  180.0 2.3 dynamic-slice_bitcast_fusion.1
  182.3 0.9 collective-permute-start.4
  183.2 4.4 %fusion.4 = f32[1792,256]{0,1:T(8,128)} fusion(bf16[1024,256]{1,0:T(8,128)(2,1)S(1)} %convolution_convert_fusion, bf16[1024,3584]{1,0:T(8,128)(2,1)} %bitcast.59), kind=kOutput, calls=%fused_computation.5 | convolution fusion | flops 939524096 | bytes 6029312 | tf_op jit(solution)/shard_map/dot_general | solution.py:19
  187.6 2.7 copy.13
  190.3 2.2 dynamic-slice_bitcast_fusion.2
  192.4 0.6 collective-permute-start.2
  193.0 0.0 copy-start.2
  193.0 11.9 %collective-permute-done.4 = f32[2,2,224,256]{3,2,1,0:T(8,128)} collective-permute-done((f32[2,2,224,256]{3,2,1,0:T(8,128)}, f32[2,2,224,256]{3,2,1,0:T(8,128)}, u32[]{:S(2)}, u32[]{:S(2)}) %collective-permute-start.4) | collective-permute-done | bytes 917536 | tf_op jit(solution)/shard_map/ppermute | solution.py:185
  205.0 1.6 bitcast_add_fusion
  206.6 0.6 collective-permute-start.5
  207.2 8.7 %collective-permute-done.2 = f32[2,2,224,256]{3,2,1,0:T(8,128)S(1)} collective-permute-done((f32[2,2,224,256]{3,2,1,0:T(8,128)}, f32[2,2,224,256]{3,2,1,0:T(8,128)S(1)}, u32[]{:S(2)}, u32[]{:S(2)}) %collective-permute-start.2) | collective-permute-done | bytes 917536 | tf_op jit(solution)/shard_map/ppermute | solution.py:185
  215.9 0.0 copy-done.2
  215.9 0.1 bitcast_add_fusion.1
  216.1 1.2 collective-permute-start.3
  217.3 7.3 %collective-permute-done.5 = f32[2,224,256]{2,1,0:T(8,128)S(1)} collective-permute-done((f32[2,224,256]{2,1,0:T(8,128)S(1)}, f32[2,224,256]{2,1,0:T(8,128)S(1)}, u32[]{:S(2)}, u32[]{:S(2)}) %collective-permute-start.5) | collective-permute-done | bytes 458784 | tf_op jit(solution)/shard_map/ppermute | solution.py:185
  224.6 0.1 bitcast_add_fusion.2
  224.7 1.8 collective-permute-done.3
  226.4 0.1 bitcast_add_fusion.3
  226.5 0.1 pad_maximum_fusion
  226.6 23.5 %all_to_all.21 = f32[4,224,256]{2,1,0:T(8,128)S(1)} all-to-all(f32[4,224,256]{2,1,0:T(8,128)S(1)} %pad_maximum_fusion), channel_id=1, replica_groups={{0,8,16,24},{2,10,18,26},{4,12,20,28},{6,14,22,30},{1,9,17,25},{3,11,19..., dimensions={0} | all-to-all | bytes 1835008 | tf_op jit(solution)/shard_map/all_to_all | solution.py:205
  250.1 0.1 reduce_sum.18.sketch
  250.1 0.1 copy.15
  250.3 0.4 fusion.18
  250.7 11.2 %all_to_all.22 = f32[16,16,256]{2,1,0:T(8,128)S(1)} all-to-all(f32[16,16,256]{2,1,0:T(8,128)S(1)} %fusion.18), channel_id=1, replica_groups=mesh['expert'=16,'dp'=2] {'expert'}, dimensions={0} | all-to-all | bytes 524288 | tf_op jit(solution)/shard_map/all_to_all | solution.py:216
  261.9 0.1 collective-permute-start.6
  262.0 1.2 collective-permute-done.6
  263.2 0.7 broadcast_in_dim.18
  263.9 3.7 %all-to-all-start.3 = ((f32[16,16,256]{2,1,0:T(8,128)}), f32[16,16,256]{2,1,0:T(8,128)S(1)}, u32[]{:S(2)}, u32[]{:S(2)}) async-start(f32[16,16,256]{2,1,0:T(8,128)} %broadcast_in_dim.18), calls=%async_computation.3 | async-start | bytes 524288 | tf_op jit(solution)/shard_map/all_to_all | solution.py:220
  267.6 3.2 %dynamic-slice_bitcast_fusion = f32[1,512,1024]{2,1,0:T(8,128)} fusion(f32[1024,1024]{1,0:T(8,128)} %copy-done.1, s32[]{:T(128)S(6)} %select_n.55), kind=kLoop, calls=%fused_computation.13 | loop fusion | bytes 4194308 | tf_op jit(solution)/shard_map/broadcast_in_dim | solution.py:259
  270.8 7.1 %all-to-all-done.3 = f32[16,16,256]{2,1,0:T(8,128)S(1)} async-done(((f32[16,16,256]{2,1,0:T(8,128)}), f32[16,16,256]{2,1,0:T(8,128)S(1)}, u32[]{:S(2)}, u32[]{:S(2)}) %all-to-all-start.3) | async-done | bytes 262176 | tf_op jit(solution)/shard_map/all_to_all | solution.py:220
  277.8 10.3 %shard_map.69 = f32[224,256]{1,0:T(8,128)} custom-call(f32[256,256]{1,0:T(8,128)S(1)} %bitcast.47, f32[224,256]{1,0:T(8,128)S(1)} %reduce_sum.18.sketch), custom_call_target="tpu_custom_call" | custom-call | tf_op jit(solution)/shard_map/pallas_call | solution.py:167
  (5 shorter events, 0.1 us)
Async XLA Ops:
  0.6 1.6 copy-start
  115.9 5.8 %collective-permute-start.1 = (f32[512,1024]{1,0:T(8,128)}, f32[512,1024]{1,0:T(8,128)}, u32[]{:S(2)}, u32[]{:S(2)}) collective-permute-start(f32[512,1024]{1,0:T(8,128)} %fusion.10.low_a), channel_id=1, source_target_pairs={{0,1},{1,0},{2,3},{3,2},{4,5},{5,4},{6,7},{7,6},{8,9},{9,8},{10,11... | collective-permute-start | bytes 6291464 | tf_op jit(solution)/shard_map/ppermute | solution.py:244
  117.2 4.5 %collective-permute-start = (f32[512,512]{1,0:T(8,128)S(1)}, f32[512,512]{1,0:T(8,128)}, u32[]{:S(2)}, u32[]{:S(2)}) collective-permute-start(f32[512,512]{1,0:T(8,128)S(1)} %fusion.12.top_a), channel_id=1, source_target_pairs={{0,1},{1,0},{2,3},{3,2},{4,5},{5,4},{6,7},{7,6},{8,9},{9,8},{10,11... | collective-permute-start | bytes 3145736 | tf_op jit(solution)/shard_map/ppermute | solution.py:246
  117.8 53.0 %copy-start.3 = (bf16[1,1024,256]{2,1,0:T(8,128)(2,1)S(1)}, bf16[1,1024,256]{2,1,0:T(8,128)(2,1)}, u32[]{:S(2)}) copy-start(bf16[1,1024,256]{2,1,0:T(8,128)(2,1)} %param.9) | copy-start | bytes 1572868
  168.9 1.9 copy-start.1
  182.3 22.7 %collective-permute-start.4 = (f32[2,2,224,256]{3,2,1,0:T(8,128)}, f32[2,2,224,256]{3,2,1,0:T(8,128)}, u32[]{:S(2)}, u32[]{:S(2)}) collective-permute-start(f32[2,2,224,256]{3,2,1,0:T(8,128)} %dynamic-slice_bitcast_fusion.1), channel_id=1, source_target_pairs={{0,4},{2,6},{4,0},{6,2},{8,12},{10,14},{12,8},{14,10},{16,20},{18,... | collective-permute-start | bytes 2752520 | tf_op jit(solution)/shard_map/ppermute | solution.py:185
  192.4 23.4 %collective-permute-start.2 = (f32[2,2,224,256]{3,2,1,0:T(8,128)}, f32[2,2,224,256]{3,2,1,0:T(8,128)S(1)}, u32[]{:S(2)}, u32[]{:S(2)}) collective-permute-start(f32[2,2,224,256]{3,2,1,0:T(8,128)} %dynamic-slice_bitcast_fusion.2), channel_id=1, source_target_pairs={{0,2},{2,0},{4,6},{6,4},{8,10},{10,8},{12,14},{14,12},{16,18},{18,... | collective-permute-start | bytes 2752520 | tf_op jit(solution)/shard_map/ppermute | solution.py:185
  193.0 22.9 %copy-start.2 = (f32[1792,256]{1,0:T(8,128)S(1)}, f32[1792,256]{1,0:T(8,128)}, u32[]{:S(2)}) copy-start(f32[1792,256]{1,0:T(8,128)} %copy.13) | copy-start | bytes 5505028
  206.6 18.0 %collective-permute-start.5 = (f32[2,224,256]{2,1,0:T(8,128)S(1)}, f32[2,224,256]{2,1,0:T(8,128)S(1)}, u32[]{:S(2)}, u32[]{:S(2)}) collective-permute-start(f32[2,224,256]{2,1,0:T(8,128)S(1)} %dynamic-slice_bitcast_fusion.3), channel_id=1, source_target_pairs={{0,2},{2,0},{4,6},{6,4},{8,10},{10,8},{12,14},{14,12},{16,18},{18,... | collective-permute-start | bytes 1376264 | tf_op jit(solution)/shard_map/ppermute | solution.py:185
  216.1 10.4 %collective-permute-start.3 = (f32[2,224,256]{2,1,0:T(8,128)S(1)}, f32[2,224,256]{2,1,0:T(8,128)S(1)}, u32[]{:S(2)}, u32[]{:S(2)}) collective-permute-start(f32[2,224,256]{2,1,0:T(8,128)S(1)} %dynamic-slice_bitcast_fusion.4), channel_id=1, source_target_pairs={{0,4},{2,6},{4,0},{6,2},{8,12},{10,14},{12,8},{14,10},{16,20},{18,... | collective-permute-start | bytes 1376264 | tf_op jit(solution)/shard_map/ppermute | solution.py:185
  261.9 1.2 collective-permute-start.6
  263.9 14.0 %all-to-all-start.3 = ((f32[16,16,256]{2,1,0:T(8,128)}), f32[16,16,256]{2,1,0:T(8,128)S(1)}, u32[]{:S(2)}, u32[]{:S(2)}) async-start(f32[16,16,256]{2,1,0:T(8,128)} %broadcast_in_dim.18), calls=%async_computation.3 | async-start | bytes 524288 | tf_op jit(solution)/shard_map/all_to_all | solution.py:220

commit v3 on v2

--- a/solution.py
+++ b/solution.py
@@ -177,6 +177,32 @@
     )(gram, sketch)
 
 
+def term_kernel(test_t, down, out):
+    out[...] = jnp.dot(test_t[...], down[...], preferred_element_type=jnp.float32).T
+
+
+def sketch_term(down_half, test_t, begin, rows):
+    rank, depth = test_t.shape
+    tile = 256
+    skip = begin // tile
+    return pl.pallas_call(
+        term_kernel,
+        grid=(rows // tile,),
+        out_shape=jax.ShapeDtypeStruct((rows, rank), jnp.float32),
+        in_specs=[
+            pl.BlockSpec((rank, depth), lambda i: (0, 0)),
+            pl.BlockSpec((depth, tile), lambda i: (0, i + skip)),
+        ],
+        out_specs=pl.BlockSpec((tile, rank), lambda i: (i, 0)),
+        cost_estimate=pl.CostEstimate(
+            flops=2 * rows * rank * depth,
+            bytes_accessed=2 * rows * depth + 4 * rows * rank,
+            transcendentals=0,
+        ),
+        compiler_params=pltpu.CompilerParams(vmem_limit_bytes=16 * 2**20),
+    )(test_t, down_half)
+
+
 def exchange(parts, bit, axis):
     mine = (lax.axis_index("expert") // bit) % 2
     pairs = [(i, i ^ bit) for i in range(lax.axis_size("expert"))]
@@ -185,16 +211,16 @@
     return kept, lax.ppermute(sent, "expert", pairs)
 
 
-def scatter_sum(down_half, test_mat, n_exp):
+def scatter_sum(down_half, test_t, n_exp):
     half_cols = down_half.shape[1]
     share = half_cols // n_exp
-    rank = test_mat.shape[1]
+    rank = test_t.shape[0]
     outer = n_exp // 4
     cut = half_cols // 2
     shape = (outer // 2, 2, 2, share, rank)
-    first = contract(down_half[:, :cut], test_mat).reshape(shape)
+    first = sketch_term(down_half, test_t, 0, cut).reshape(shape)
     first_kept, first_came = exchange(first, 1, 2)
-    second = contract(down_half[:, cut:], test_mat).reshape(shape)
+    second = sketch_term(down_half, test_t, cut, cut).reshape(shape)
     second_kept, second_came = exchange(second, 2, 1)
     first = first_kept + first_came
     first_kept, first_came = exchange(first, 2, 1)
@@ -245,12 +271,12 @@
     top = contract(received[:, :half], received[:, :half])
     top_other = lax.ppermute(top, "dp", swap)
     whitening = whiten(n_slot, top, top_other, low, low_other)
-    test_mat = jnp.dot(
-        whitening, omega[0].astype(jnp.float32), precision=HIGH
+    test_t = lax.dot_general(
+        omega[0].astype(jnp.float32), whitening, (((0,), (1,)), ((), ())), precision=HIGH
     ).astype(jnp.bfloat16)
     down_half = down_weight[0]
     half_cols = down_half.shape[1]
-    sketch = scatter_sum(down_half, test_mat, n_exp)
+    sketch = scatter_sum(down_half, test_t, n_exp)
     small_gram = gram_over_all(sketch, n_exp, swap)
     basis_rows = finish(math.sqrt(half_cols * n_dp), small_gram, sketch)
     own_rows = lax.dynamic_slice_in_dim(

time: 289 us -> 286 us (0.990)
  matrix products: 16.2 us -> 7.57 us
  Pallas kernels: 57.4 us -> 63.3 us
    dot_general x4 -> x2, matrix products: 13.8 us -> 4.96 us  [contract(): lax.dot_general(left, right, (((0,), (0,)), ((), ())), preferred_element_...]
    unnamed x8 -> x16, local copies, waits for them, and re-layouts: 2.48 us -> 9.19 us
    pallas_call x0 -> x2, Pallas kernels: none -> 5.83 us  [sketch_term(): pl.pallas_call(term_kernel, grid=(rows // tile,), out_shape=jax.ShapeDtyp...]
    dot_general x2 -> x0, local copies, waits for them, and re-layouts: 5.47 us -> none  [contract(): lax.dot_general(left, right, (((0,), (0,)), ((), ())), preferred_element_...]
  transfers between devices with their start and end apart: 8 -> 8, of which waited for: 7 -> 7; matrix products, arithmetic and copies ran while one was open for 5% -> 3% of each run, Pallas kernels for 0% -> 1%
where the time goes in v3:
time: 286 us; the launch traced here: 285 us
  blocking collectives  136 us (48%)
  Pallas kernels  63.3 us (22%)
  waiting for transfers between devices  42.4 us (15%)
  local copies, waits for them, and re-layouts  23.5 us (8%)
  matrix products  7.57 us (3%)
  starting transfers between devices  7.52 us (3%)
  other arithmetic  3.72 us (1%)
    all_to_all x1, blocking collectives, local(): lax.all_to_all(outgoing, 'expert', split_axis=0, concat_axis=0, tiled=True)  102 us
    pallas_call x1, Pallas kernels, whiten(): pl.pallas_call(functools.partial(whiten_kernel, n_slot), out_shape=jax.Sh...  47.2 us
    ppermute x4, waiting for transfers between devices, exchange(): return (kept, lax.ppermute(sent, 'expert', pairs))  30.1 us
    all_to_all x1, blocking collectives, scatter_sum(): lax.all_to_all(quarter, 'expert', split_axis=0, concat_axis=0, axis_index...  23.2 us
    all_to_all x1, blocking collectives, gram_over_all(): lax.all_to_all(pieces, 'expert', split_axis=0, concat_axis=0, tiled=True)  11.2 us
    pallas_call x1, Pallas kernels, finish(): pl.pallas_call(functools.partial(basis_kernel, root), out_shape=jax.Shape...  10.3 us
    unnamed x16, local copies, waits for them, and re-layouts  9.19 us
    scatter x1, local copies, waits for them, and re-layouts, local(): outgoing = outgoing.at[slot_index].set(hidden.reshape(-1, hid_width)).res...  7.9 us
  transfers between devices with their start and end apart: 8, of which 7 were waited for; matrix products, arithmetic and copies ran while one was open for 3% of the time, Pallas kernels for 1%

profile of v3, /device:TPU:0, one launch (start us, length us, event | category | flops | bytes accessed | tf_op | source)
XLA Modules:
  0.0 285.2 jit_solution(10650407040118966482)
XLA Ops:
  0.6 0.0 copy-start
  0.6 0.9 multiply_add_fusion
  1.5 0.1 copy.9
  1.6 0.1 reshape.56
  1.7 0.5 copy-done
  2.3 7.9 %scatter_custom_fusion = bf16[2048,1024]{1,0:T(8,128)(2,1)} fusion(s32[1024]{0:T(1024)S(1)} %bitcast.55, bf16[128,8,1024]{2,1,0:T(8,128)(2,1)S(1)} %copy-done, bf16[]{:T(256)} %constant.79.clone.1), kind=kCustom, calls=%fused_computation.5 | custom fusion | bytes 6291458 | tf_op jit(solution)/shard_map/scatter | solution.py:261
  10.2 102.1 %all_to_all.20 = bf16[16,128,1024]{2,1,0:T(8,128)(2,1)S(1)} all-to-all(bf16[16,128,1024]{2,1,0:T(8,128)(2,1)} %bitcast.50), channel_id=1, replica_groups=mesh['expert'=16,'dp'=2] {'expert'}, dimensions={0} | all-to-all | bytes 8388608 | tf_op jit(solution)/shard_map/all_to_all | solution.py:264
  112.3 3.7 %fusion.low_a = f32[512,1024]{1,0:T(8,128)} fusion(bf16[2048,1024]{1,0:T(8,128)(2,1)S(1)} %bitcast.51), kind=kOutput, calls=%fused_computation.1 | convolution fusion | flops 2147483648 | bytes 8388608 | tf_op jit(solution)/shard_map/dot_general | solution.py:19
  115.9 0.0 collective-permute-start.1
  115.9 1.3 fusion.2.top_a
  117.2 0.6 collective-permute-start
  117.8 0.0 copy-start.7
  117.8 3.9 %collective-permute-done.top_b = f32[512,512]{1,0:T(8,128)} collective-permute-done((f32[512,512]{1,0:T(8,128)S(1)}, f32[512,512]{1,0:T(8,128)}, u32[]{:S(2)}, u32[]{:S(2)}) %collective-permute-start) | collective-permute-done | bytes 1048608 | tf_op jit(solution)/shard_map/ppermute | solution.py:272
  121.7 0.0 collective-permute-done.1.low_b
  121.7 47.2 %shard_map.68 = f32[1024,1024]{1,0:T(8,128)S(1)} custom-call(f32[512,512]{1,0:T(8,128)S(1)} %fusion.2.top_a, f32[512,512]{1,0:T(8,128)} %collective-permute-done.top_b, f32[512,1024]{1,0:T(8,128)} %fusion.low_a, f32[512,1024]{1,0:T(8,128)} %collective-permute-done.1.low_b), custom_call_target="tpu_custom_call" | custom-call | tf_op jit(solution)/shard_map/pallas_call | solution.py:156
  168.9 0.0 copy-done.7
  168.9 0.0 copy-start.3
  168.9 2.2 fusion.7.test_t
  171.2 0.0 copy-done.3
  171.2 0.0 copy-start.1
  171.2 3.1 %copy-done.1 = bf16[1,1024,3584]{2,1,0:T(8,128)(2,1)S(1)} copy-done((bf16[1,1024,3584]{2,1,0:T(8,128)(2,1)S(1)}, bf16[1,1024,3584]{2,1,0:T(8,128)(2,1)}, u32[]{:S(2)}) %copy-start.1) | copy-done | bytes 7340056
  174.3 2.9 %shard_map.70 = f32[1792,256]{1,0:T(8,128)S(1)} custom-call(bf16[256,1024]{1,0:T(8,128)(2,1)S(1)} %fusion.7.test_t, bf16[1024,3584]{1,0:T(8,128)(2,1)S(1)} %bitcast.42), custom_call_target="tpu_custom_call" | custom-call | flops 939524096 | bytes 5505024 | tf_op jit(solution)/shard_map/pallas_call | solution.py:188
  177.2 0.0 copy-start.4
  177.2 1.2 copy-done.4
  178.4 1.0 dynamic-slice_bitcast_fusion.1
  179.4 0.9 collective-permute-start.4
  180.3 0.0 copy-start.2
  180.3 3.1 %copy-done.2 = bf16[1,1024,3584]{2,1,0:T(8,128)(2,1)S(1)} copy-done((bf16[1,1024,3584]{2,1,0:T(8,128)(2,1)S(1)}, bf16[1,1024,3584]{2,1,0:T(8,128)(2,1)}, u32[]{:S(2)}) %copy-start.2) | copy-done | bytes 7340056
  183.4 2.9 %shard_map.69 = f32[1792,256]{1,0:T(8,128)S(1)} custom-call(bf16[256,1024]{1,0:T(8,128)(2,1)S(1)} %fusion.7.test_t, bf16[1024,3584]{1,0:T(8,128)(2,1)S(1)} %bitcast.43), custom_call_target="tpu_custom_call" | custom-call | flops 939524096 | bytes 5505024 | tf_op jit(solution)/shard_map/pallas_call | solution.py:188
  186.3 0.0 copy-start.5
  186.3 1.2 copy-done.5
  187.6 1.1 dynamic-slice_bitcast_fusion.2
  188.6 0.6 collective-permute-start.2
  189.2 0.0 copy-start.6
  189.2 12.8 %collective-permute-done.4 = f32[2,2,224,256]{3,2,1,0:T(8,128)S(1)} collective-permute-done((f32[2,2,224,256]{3,2,1,0:T(8,128)}, f32[2,2,224,256]{3,2,1,0:T(8,128)S(1)}, u32[]{:S(2)}, u32[]{:S(2)}) %collective-permute-start.4) | collective-permute-done | bytes 917536 | tf_op jit(solution)/shard_map/ppermute | solution.py:211
  202.0 1.3 bitcast_add_fusion
  203.3 0.6 collective-permute-start.5
  204.0 8.2 %collective-permute-done.2 = f32[2,2,224,256]{3,2,1,0:T(8,128)} collective-permute-done((f32[2,2,224,256]{3,2,1,0:T(8,128)}, f32[2,2,224,256]{3,2,1,0:T(8,128)}, u32[]{:S(2)}, u32[]{:S(2)}) %collective-permute-start.2) | collective-permute-done | bytes 917536 | tf_op jit(solution)/shard_map/ppermute | solution.py:211
  212.2 0.0 copy-done.6
  212.2 1.3 bitcast_add_fusion.1
  213.5 1.2 collective-permute-start.3
  214.7 6.1 %collective-permute-done.5 = f32[2,224,256]{2,1,0:T(8,128)S(1)} collective-permute-done((f32[2,224,256]{2,1,0:T(8,128)S(1)}, f32[2,224,256]{2,1,0:T(8,128)S(1)}, u32[]{:S(2)}, u32[]{:S(2)}) %collective-permute-start.5) | collective-permute-done | bytes 458784 | tf_op jit(solution)/shard_map/ppermute | solution.py:211
  220.8 0.1 bitcast_add_fusion.2
  220.9 3.0 %collective-permute-done.3 = f32[2,224,256]{2,1,0:T(8,128)S(1)} collective-permute-done((f32[2,224,256]{2,1,0:T(8,128)S(1)}, f32[2,224,256]{2,1,0:T(8,128)S(1)}, u32[]{:S(2)}, u32[]{:S(2)}) %collective-permute-start.3) | collective-permute-done | bytes 458784 | tf_op jit(solution)/shard_map/ppermute | solution.py:211
  223.9 0.1 bitcast_add_fusion.3
  224.0 0.1 pad_maximum_fusion
  224.0 23.2 %all_to_all.21 = f32[4,224,256]{2,1,0:T(8,128)S(1)} all-to-all(f32[4,224,256]{2,1,0:T(8,128)S(1)} %pad_maximum_fusion), channel_id=1, replica_groups={{0,8,16,24},{2,10,18,26},{4,12,20,28},{6,14,22,30},{1,9,17,25},{3,11,19..., dimensions={0} | all-to-all | bytes 1835008 | tf_op jit(solution)/shard_map/all_to_all | solution.py:231
  247.2 0.1 reduce_sum.18.sketch
  247.3 0.1 copy.11
  247.4 0.4 fusion.9
  247.8 11.2 %all_to_all.22 = f32[16,16,256]{2,1,0:T(8,128)S(1)} all-to-all(f32[16,16,256]{2,1,0:T(8,128)S(1)} %fusion.9), channel_id=1, replica_groups=mesh['expert'=16,'dp'=2] {'expert'}, dimensions={0} | all-to-all | bytes 524288 | tf_op jit(solution)/shard_map/all_to_all | solution.py:242
  259.0 0.1 collective-permute-start.6
  259.1 1.2 collective-permute-done.6
  260.2 0.7 broadcast_in_dim.18
  261.0 3.6 %all-to-all-start.3 = ((f32[16,16,256]{2,1,0:T(8,128)}), f32[16,16,256]{2,1,0:T(8,128)S(1)}, u32[]{:S(2)}, u32[]{:S(2)}) async-start(f32[16,16,256]{2,1,0:T(8,128)} %broadcast_in_dim.18), calls=%async_computation.3 | async-start | bytes 524288 | tf_op jit(solution)/shard_map/all_to_all | solution.py:246
  264.6 3.2 %dynamic-slice_bitcast_fusion = f32[1,512,1024]{2,1,0:T(8,128)} fusion(f32[1024,1024]{1,0:T(8,128)} %copy-done.3, s32[]{:T(128)S(6)} %select_n.55), kind=kLoop, calls=%fused_computation.7 | loop fusion | bytes 4194308 | tf_op jit(solution)/shard_map/broadcast_in_dim | solution.py:285
  267.7 7.2 %all-to-all-done.3 = f32[16,16,256]{2,1,0:T(8,128)S(1)} async-done(((f32[16,16,256]{2,1,0:T(8,128)}), f32[16,16,256]{2,1,0:T(8,128)S(1)}, u32[]{:S(2)}, u32[]{:S(2)}) %all-to-all-start.3) | async-done | bytes 262176 | tf_op jit(solution)/shard_map/all_to_all | solution.py:246
  274.9 10.3 %shard_map.71 = f32[224,256]{1,0:T(8,128)} custom-call(f32[256,256]{1,0:T(8,128)S(1)} %bitcast.49, f32[224,256]{1,0:T(8,128)S(1)} %reduce_sum.18.sketch), custom_call_target="tpu_custom_call" | custom-call | tf_op jit(solution)/shard_map/pallas_call | solution.py:167
  (5 shorter events, 0.1 us)
Async XLA Ops:
  0.6 1.6 copy-start
  115.9 5.8 %collective-permute-start.1 = (f32[512,1024]{1,0:T(8,128)}, f32[512,1024]{1,0:T(8,128)}, u32[]{:S(2)}, u32[]{:S(2)}) collective-permute-start(f32[512,1024]{1,0:T(8,128)} %fusion.low_a), channel_id=1, source_target_pairs={{0,1},{1,0},{2,3},{3,2},{4,5},{5,4},{6,7},{7,6},{8,9},{9,8},{10,11... | collective-permute-start | bytes 6291464 | tf_op jit(solution)/shard_map/ppermute | solution.py:270
  117.2 4.5 %collective-permute-start = (f32[512,512]{1,0:T(8,128)S(1)}, f32[512,512]{1,0:T(8,128)}, u32[]{:S(2)}, u32[]{:S(2)}) collective-permute-start(f32[512,512]{1,0:T(8,128)S(1)} %fusion.2.top_a), channel_id=1, source_target_pairs={{0,1},{1,0},{2,3},{3,2},{4,5},{5,4},{6,7},{7,6},{8,9},{9,8},{10,11... | collective-permute-start | bytes 3145736 | tf_op jit(solution)/shard_map/ppermute | solution.py:272
  117.8 51.1 %copy-start.7 = (bf16[1,1024,256]{2,1,0:T(8,128)(2,1)S(1)}, bf16[1,1024,256]{2,1,0:T(8,128)(2,1)}, u32[]{:S(2)}) copy-start(bf16[1,1024,256]{2,1,0:T(8,128)(2,1)} %param.9) | copy-start | bytes 1572868
  168.9 2.2 copy-start.3
  171.2 3.1 %copy-start.1 = (bf16[1,1024,3584]{2,1,0:T(8,128)(2,1)S(1)}, bf16[1,1024,3584]{2,1,0:T(8,128)(2,1)}, u32[]{:S(2)}) copy-start(bf16[1,1024,3584]{2,1,0:T(8,128)(2,1)} %param.8) | copy-start | bytes 22020100
  177.2 1.2 copy-start.4
  179.4 22.6 %collective-permute-start.4 = (f32[2,2,224,256]{3,2,1,0:T(8,128)}, f32[2,2,224,256]{3,2,1,0:T(8,128)S(1)}, u32[]{:S(2)}, u32[]{:S(2)}) collective-permute-start(f32[2,2,224,256]{3,2,1,0:T(8,128)} %dynamic-slice_bitcast_fusion.1), channel_id=1, source_target_pairs={{0,4},{2,6},{4,0},{6,2},{8,12},{10,14},{12,8},{14,10},{16,20},{18,... | collective-permute-start | bytes 2752520 | tf_op jit(solution)/shard_map/ppermute | solution.py:211
  180.3 3.1 %copy-start.2 = (bf16[1,1024,3584]{2,1,0:T(8,128)(2,1)S(1)}, bf16[1,1024,3584]{2,1,0:T(8,128)(2,1)}, u32[]{:S(2)}) copy-start(bf16[1,1024,3584]{2,1,0:T(8,128)(2,1)} %param.8) | copy-start | bytes 22020100
  186.3 1.3 copy-start.5
  188.6 23.6 %collective-permute-start.2 = (f32[2,2,224,256]{3,2,1,0:T(8,128)}, f32[2,2,224,256]{3,2,1,0:T(8,128)}, u32[]{:S(2)}, u32[]{:S(2)}) collective-permute-start(f32[2,2,224,256]{3,2,1,0:T(8,128)} %dynamic-slice_bitcast_fusion.2), channel_id=1, source_target_pairs={{0,2},{2,0},{4,6},{6,4},{8,10},{10,8},{12,14},{14,12},{16,18},{18,... | collective-permute-start | bytes 2752520 | tf_op jit(solution)/shard_map/ppermute | solution.py:211
  189.2 23.0 %copy-start.6 = (f32[1792,256]{1,0:T(8,128)S(1)}, f32[1792,256]{1,0:T(8,128)}, u32[]{:S(2)}) copy-start(f32[1792,256]{1,0:T(8,128)} %copy-done.5) | copy-start | bytes 5505028
  203.3 17.5 %collective-permute-start.5 = (f32[2,224,256]{2,1,0:T(8,128)S(1)}, f32[2,224,256]{2,1,0:T(8,128)S(1)}, u32[]{:S(2)}, u32[]{:S(2)}) collective-permute-start(f32[2,224,256]{2,1,0:T(8,128)S(1)} %dynamic-slice_bitcast_fusion.3), channel_id=1, source_target_pairs={{0,2},{2,0},{4,6},{6,4},{8,10},{10,8},{12,14},{14,12},{16,18},{18,... | collective-permute-start | bytes 1376264 | tf_op jit(solution)/shard_map/ppermute | solution.py:211
  213.5 10.4 %collective-permute-start.3 = (f32[2,224,256]{2,1,0:T(8,128)S(1)}, f32[2,224,256]{2,1,0:T(8,128)S(1)}, u32[]{:S(2)}, u32[]{:S(2)}) collective-permute-start(f32[2,224,256]{2,1,0:T(8,128)S(1)} %dynamic-slice_bitcast_fusion.4), channel_id=1, source_target_pairs={{0,4},{2,6},{4,0},{6,2},{8,12},{10,14},{12,8},{14,10},{16,20},{18,... | collective-permute-start | bytes 1376264 | tf_op jit(solution)/shard_map/ppermute | solution.py:211
  259.0 1.2 collective-permute-start.6
  261.0 14.0 %all-to-all-start.3 = ((f32[16,16,256]{2,1,0:T(8,128)}), f32[16,16,256]{2,1,0:T(8,128)S(1)}, u32[]{:S(2)}, u32[]{:S(2)}) async-start(f32[16,16,256]{2,1,0:T(8,128)} %broadcast_in_dim.18), calls=%async_computation.3 | async-start | bytes 524288 | tf_op jit(solution)/shard_map/all_to_all | solution.py:246
